TPU v7x, 32 devices: a whole 2x2x4 slice. The times are simulated.
32 devices in a mesh: row: 8 (over z, core), col: 4 (over y, x).
Axes of the slice: x: 2, y: 2, z: 4, core: 2. Of those that a mesh axis runs over, the one named last changes fastest.
Arguments:
- diag_rows: bfloat16 [8, 16, 512, 512], P('row', 'col'), may hold values from -0.12988281 to 0.12988281
- next_rows: bfloat16 [8, 16, 128, 512], P('row', 'col'), may hold values from -6 to 6
- routes: int32 [8, 4, 4], P('row', 'col'), may hold values from 0 to 3, each once within a row
- diag_blocks: bfloat16 [8, 4, 512, 512], P('row', 'col'), as said below
- panel_blocks: bfloat16 [8, 4, 128, 512], P('row', 'col'), may hold values from -6 to 6
Outputs:
- diag_factor: bfloat16 [8, 4, 512, 512], P('row', 'col')
- panel_factor: bfloat16 [8, 4, 128, 512], P('row', 'col')
Inputs may be any that keep to these rules, and one draw needn't show every extreme that they name: `routes`: the 4 sources of one device name every target column exactly once. `diag_blocks`: every block is symmetric positive definite with eigenvalues of at least 0.5 before rounding.
All inputs are finite; a program needn't handle non-finite values.
Results may differ from a plain program's by a relative error of at most 0.001.
Values may be sent and summed in bfloat16 or wider, within the bound.
A program may use at most 128 MiB of HBM per device.

v0:
```python
import jax
import jax.numpy as jnp
from jax import lax
from jax.sharding import PartitionSpec as P


def from_behind(value, axis, steps):
    count = lax.axis_size(axis)
    pairs = [(source, (source + steps) % count) for source in range(count)]
    return lax.ppermute(value, axis, pairs)


def place_slots(sources, targets, columns):
    selector = (targets[0, 0, :][:, None] == jnp.arange(columns, dtype=jnp.int32)[None, :]).astype(
        jnp.bfloat16
    )
    placed = jnp.einsum("sj,sab->jab", selector, sources, preferred_element_type=jnp.float32)
    return placed.astype(jnp.bfloat16)


def block_sum(left_slots, right_slots):
    return jnp.einsum("cik,cjk->ij", left_slots, right_slots, preferred_element_type=jnp.float32)


def solve_panel(factor, total):
    return jax.scipy.linalg.solve_triangular(factor, total.T, lower=True).T


def body(diag_rows, next_rows, routes, diag_blocks, panel_blocks):
    columns = lax.axis_size("col")
    send_diag = place_slots(diag_rows[0], routes, columns)
    lifted_next, panel_source = from_behind((next_rows, panel_blocks), "row", -1)
    send_next = place_slots(lifted_next[0], routes, columns)
    recv_diag, recv_next = (
        lax.all_to_all(send_diag, "col", split_axis=0, concat_axis=0, tiled=True),
        lax.all_to_all(send_next, "col", split_axis=0, concat_axis=0, tiled=True),
    )
    factor = jnp.linalg.cholesky(
        diag_blocks[0, 0].astype(jnp.float32) + block_sum(recv_diag, recv_diag)
    )
    total = panel_source[0, 0].astype(jnp.float32) + block_sum(recv_next, recv_diag)
    solved = solve_panel(factor, total).astype(jnp.bfloat16)
    panel_out = from_behind(solved, "row", 1)
    return (factor.astype(jnp.bfloat16)[None, None], panel_out[None, None])


def solution(mesh):
    placed = (
        P("row", "col", None, None),
        P("row", "col", None, None),
        P("row", "col", None),
        P("row", "col", None, None),
        P("row", "col", None, None),
    )
    return jax.shard_map(
        body,
        mesh=mesh,
        in_specs=placed,
        out_specs=(P("row", "col", None, None), P("row", "col", None, None)),
        check_vma=False,
    )
```

profile of v0, /device:TPU:0, one launch (start us, length us, event | category | flops | bytes accessed | tf_op | source)
XLA Modules:
  0.0 208.8 jit_solution(1055346275551178674)
XLA Ops:
  0.6 1.6 copy-done
  2.2 2.4 %fusion.2 = bf16[4,512,512]{2,0,1:T(4,128)(2,1)S(1)} fusion(bf16[4,512,512]{2,1,0:T(8,128)(2,1)S(1)} %bitcast.83, s32[4]{0:T(128)} %bitcast.85), kind=kOutput, calls=%fused_computation.4 | convolution fusion | flops 9437200 | bytes 4194320 | tf_op jit(solution)/shard_map/sj,sab->jab/dot_general | solution.py:17
  4.6 1.7 copy.17
  6.3 5.3 %all-to-all-start = ((bf16[4,512,512]{2,1,0:T(8,128)(2,1)}), bf16[4,512,512]{2,1,0:T(8,128)(2,1)}, u32[]{:S(2)}, u32[]{:S(2)}) async-start(bf16[4,512,512]{2,1,0:T(8,128)(2,1)} %copy.17), calls=%async_computation | async-start | bytes 4194304 | tf_op jit(solution)/shard_map/all_to_all | solution.py:35
  11.6 3.8 %collective-permute-start.1 = (bf16[1,4,128,512]{3,2,1,0:T(8,128)(2,1)S(1)}, bf16[1,4,128,512]{3,2,1,0:T(8,128)(2,1)}, u32[]{:S(2)}, u32[]{:S(2)}) collective-permute-start(bf16[1,4,128,512]{3,2,1,0:T(8,128)(2,1)S(1)} %copy-done.3), channel_id=1, source_target_pairs={{0,28},{4,0},{8,4},{12,8},{16,12},{20,16},{24,20},{28,24},{1,29},{... | collective-permute-start | bytes 1572872 | tf_op jit(solution)/shard_map/ppermute | solution.py:10
  15.4 0.7 collective-permute-start
  16.1 1.0 copy.15
  17.1 5.0 %collective-permute-done.1 = bf16[1,4,128,512]{3,2,1,0:T(8,128)(2,1)} collective-permute-done((bf16[1,4,128,512]{3,2,1,0:T(8,128)(2,1)S(1)}, bf16[1,4,128,512]{3,2,1,0:T(8,128)(2,1)}, u32[]{:S(2)}, u32[]{:S(2)}) %collective-permute-start.1) | collective-permute-done | bytes 524320 | tf_op jit(solution)/shard_map/ppermute | solution.py:10
  22.1 1.5 fusion.10
  23.7 0.9 copy.32
  24.5 12.8 %all-to-all-done = bf16[4,512,512]{2,1,0:T(8,128)(2,1)} async-done(((bf16[4,512,512]{2,1,0:T(8,128)(2,1)}), bf16[4,512,512]{2,1,0:T(8,128)(2,1)}, u32[]{:S(2)}, u32[]{:S(2)}) %all-to-all-start) | async-done | bytes 2097184 | tf_op jit(solution)/shard_map/all_to_all | solution.py:35
  37.3 4.3 %all-to-all-start.1 = ((bf16[4,128,512]{2,1,0:T(8,128)(2,1)}), bf16[4,128,512]{2,1,0:T(8,128)(2,1)}, u32[]{:S(2)}, u32[]{:S(2)}) async-start(bf16[4,128,512]{2,1,0:T(8,128)(2,1)} %copy.32), calls=%async_computation.1 | async-start | bytes 1048576 | tf_op jit(solution)/shard_map/all_to_all | solution.py:36
  41.6 3.6 %fusion.5 = f32[512,512]{0,1:T(8,128)S(1)} fusion(bf16[4,512,512]{2,1,0:T(8,128)(2,1)} %all-to-all-done, bf16[1,1,512,512]{2,3,1,0:T(8,128)(2,1)} %copy.15), kind=kOutput, calls=%fused_computation.6 | convolution fusion | flops 1074266112 | bytes 3670016 | tf_op jit(solution)/shard_map/cik,cjk->ij/dot_general | solution.py:22
  45.2 1.3 copy.19
  46.6 1.4 fusion.6
  48.0 1.0 copy-done.1
  49.0 11.7 %cholesky.104 = f32[128,128]{1,0:T(8,128)S(1)} custom-call(f32[128,128]{1,0:T(8,128)S(1)} %cholesky.266), custom_call_target="Cholesky" | custom-call | tf_op jit(solution)/shard_map/jit(cholesky)/cholesky | solution.py:38
  60.9 9.8 %custom-call.31 = f32[1,128,128]{1,2,0:T(8,128)S(1)} custom-call(f32[1,128,128]{2,1,0:T(8,128)S(1)} %get-tuple-element.33), custom_call_target="InvertDiagBlocksLowerTriangular" | custom-call | tf_op jit(solution)/shard_map/jit(cholesky)/cholesky | solution.py:38
  70.7 1.2 constant_dynamic-update-slice_fusion.3
  71.9 1.3 convolution_subtract_fusion
  73.2 0.6 cholesky.270
  73.8 12.5 %cholesky.217 = f32[128,128]{1,0:T(8,128)S(1)} custom-call(f32[128,128]{1,0:T(8,128)} %cholesky.270), custom_call_target="Cholesky" | custom-call | tf_op jit(solution)/shard_map/jit(cholesky)/cholesky | solution.py:38
  86.4 0.6 select_reduce_fusion.2
  87.0 10.8 %custom-call.32 = f32[1,128,128]{1,2,0:T(8,128)S(1)} custom-call(f32[1,128,128]{2,1,0:T(8,128)} %get-tuple-element.30), custom_call_target="InvertDiagBlocksLowerTriangular" | custom-call | tf_op jit(solution)/shard_map/jit(cholesky)/cholesky | solution.py:38
  98.1 1.3 convolution_subtract_fusion.1
  99.4 11.7 %cholesky.238 = f32[128,128]{1,0:T(8,128)S(1)} custom-call(f32[128,128]{1,0:T(8,128)S(1)} %cholesky.275), custom_call_target="Cholesky" | custom-call | tf_op jit(solution)/shard_map/jit(cholesky)/cholesky | solution.py:38
  111.2 9.8 %custom-call.33 = f32[1,128,128]{1,2,0:T(8,128)S(1)} custom-call(f32[1,128,128]{2,1,0:T(8,128)S(1)} %get-tuple-element.27), custom_call_target="InvertDiagBlocksLowerTriangular" | custom-call | tf_op jit(solution)/shard_map/jit(cholesky)/cholesky | solution.py:38
  121.2 1.2 convolution_subtract_fusion.2
  122.4 11.9 %cholesky.255 = f32[128,128]{1,0:T(8,128)S(1)} custom-call(f32[128,128]{1,0:T(8,128)S(1)} %convolution_subtract_fusion.2), custom_call_target="Cholesky" | custom-call | tf_op jit(solution)/shard_map/jit(cholesky)/cholesky | solution.py:38
  134.4 0.6 compare_reduce_fusion.1
  135.0 0.7 compare_reduce_fusion
  135.7 0.6 compare_reduce_fusion.2
  138.9 1.1 fusion.7
  140.0 14.0 %while.1 = (s32[]{:T(128)}, f32[512,512]{1,0:T(8,128)}, s32[4,2]{0,1:T(2,128)S(1)}, f32[4,128,128]{2,1,0:T(8,128)}, s32[]{:T(128)}) while((s32[]{:T(128)}, f32[512,512]{1,0:T(8,128)}, s32[4,2]{0,1:T(2,128)S(1)}, f32[4,128,128]{2,1,0:T(8,128)}, s32[]{:T(128)}) %tuple.36), condition=%wide.while_cond, body=%wide.while_body.sunk | while | flops 2 | bytes 132205 | solution.py:26
  140.6 2.9 %bitcast_dynamic-update-slice_fusion.2 = f32[4,128,128]{2,1,0:T(8,128)} fusion(f32[4,128,128]{2,1,0:T(8,128)} %get-tuple-element.81, s32[]{:T(128)S(6)} %copy.42, f32[512,512]{1,0:T(8,128)} %get-tuple-element.84, s32[]{:T(128)} %bitcast.81, s32[]{:T(128)} %bitcast.82), kind=kLoop, calls=%fused_computation.clone.1 | loop fusion | bytes 132100 | tf_op jit(solution)/shard_map/jit(_solve_triangular)/triangular_solve
  143.6 0.5 fusion.60
  144.1 2.9 %bitcast_dynamic-update-slice_fusion.2 = f32[4,128,128]{2,1,0:T(8,128)} fusion(f32[4,128,128]{2,1,0:T(8,128)} %get-tuple-element.81, s32[]{:T(128)S(6)} %copy.42, f32[512,512]{1,0:T(8,128)} %get-tuple-element.84, s32[]{:T(128)} %bitcast.81, s32[]{:T(128)} %bitcast.82), kind=kLoop, calls=%fused_computation.clone.1 | loop fusion | bytes 132100 | tf_op jit(solution)/shard_map/jit(_solve_triangular)/triangular_solve
  147.1 0.5 fusion.60
  147.6 2.9 %bitcast_dynamic-update-slice_fusion.2 = f32[4,128,128]{2,1,0:T(8,128)} fusion(f32[4,128,128]{2,1,0:T(8,128)} %get-tuple-element.81, s32[]{:T(128)S(6)} %copy.42, f32[512,512]{1,0:T(8,128)} %get-tuple-element.84, s32[]{:T(128)} %bitcast.81, s32[]{:T(128)} %bitcast.82), kind=kLoop, calls=%fused_computation.clone.1 | loop fusion | bytes 132100 | tf_op jit(solution)/shard_map/jit(_solve_triangular)/triangular_solve
  151.1 2.8 %bitcast_dynamic-update-slice_fusion.2 = f32[4,128,128]{2,1,0:T(8,128)} fusion(f32[4,128,128]{2,1,0:T(8,128)} %get-tuple-element.81, s32[]{:T(128)S(6)} %copy.42, f32[512,512]{1,0:T(8,128)} %get-tuple-element.84, s32[]{:T(128)} %bitcast.81, s32[]{:T(128)} %bitcast.82), kind=kLoop, calls=%fused_computation.clone.1 | loop fusion | bytes 132100 | tf_op jit(solution)/shard_map/jit(_solve_triangular)/triangular_solve
  154.0 40.1 %custom-call.34 = f32[4,128,128]{1,2,0:T(8,128)S(1)} custom-call(f32[4,128,128]{2,1,0:T(8,128)} %get-tuple-element.9), custom_call_target="InvertDiagBlocksLowerTriangular" | custom-call | tf_op jit(solution)/shard_map/jit(_solve_triangular)/triangular_solve | solution.py:26
  194.1 2.6 %fusion.13 = f32[512,128]{0,1:T(8,128)S(1)} fusion(bf16[1,1,128,512]{3,2,1,0:T(8,128)(2,1)S(1)} %collective-permute-done, bf16[4,128,512]{2,1,0:T(8,128)(2,1)} %all-to-all-done.1, bf16[4,512,512]{2,1,0:T(8,128)(2,1)} %all-to-all-done), kind=kOutput, calls=%fused_computation.26 | convolution fusion | flops 268566528 | bytes 3014656 | tf_op jit(solution)/shard_map/cik,cjk->ij/dot_general | solution.py:22
  197.0 1.1 fusion.32
  198.4 1.3 fusion.24
  200.0 1.4 fusion.14
  201.8 0.9 fusion.9
  202.7 5.3 %collective-permute-done.2 = bf16[128,512]{0,1:T(8,128)(2,1)S(1)} collective-permute-done((bf16[128,512]{0,1:T(8,128)(2,1)S(1)}, bf16[128,512]{0,1:T(8,128)(2,1)S(1)}, u32[]{:S(2)}, u32[]{:S(2)}) %collective-permute-start.2) | collective-permute-done | bytes 131104 | tf_op jit(solution)/shard_map/ppermute | solution.py:10
  208.0 0.8 copy.20
  (33 shorter events, 3.3 us)
Async XLA Ops:
  0.6 1.6 copy-start
  6.3 5.3 %copy-start.3 = (bf16[1,4,128,512]{3,2,1,0:T(8,128)(2,1)S(1)}, bf16[1,4,128,512]{3,2,1,0:T(8,128)(2,1)}, u32[]{:S(2)}) copy-start(bf16[1,4,128,512]{3,2,1,0:T(8,128)(2,1)} %param.6) | copy-start | bytes 1572868
  6.3 9.8 %copy-start.2 = (bf16[1,1,512,512]{3,2,1,0:T(8,128)(2,1)S(1)}, bf16[1,1,512,512]{3,2,1,0:T(8,128)(2,1)}, u32[]{:S(2)}) copy-start(bf16[1,1,512,512]{3,2,1,0:T(8,128)(2,1)} %param.8) | copy-start | bytes 1572868
  6.3 15.8 %copy-start.4 = (s32[1,1,4]{2,1,0:T(1,128)S(1)}, s32[1,1,4]{2,1,0:T(1,128)}, u32[]{:S(2)}) copy-start(s32[1,1,4]{2,1,0:T(1,128)} %param.7) | copy-start | bytes 52
  6.3 31.0 %all-to-all-start = ((bf16[4,512,512]{2,1,0:T(8,128)(2,1)}), bf16[4,512,512]{2,1,0:T(8,128)(2,1)}, u32[]{:S(2)}, u32[]{:S(2)}) async-start(bf16[4,512,512]{2,1,0:T(8,128)(2,1)} %copy.17), calls=%async_computation | async-start | bytes 4194304 | tf_op jit(solution)/shard_map/all_to_all | solution.py:35
  11.6 10.5 %collective-permute-start.1 = (bf16[1,4,128,512]{3,2,1,0:T(8,128)(2,1)S(1)}, bf16[1,4,128,512]{3,2,1,0:T(8,128)(2,1)}, u32[]{:S(2)}, u32[]{:S(2)}) collective-permute-start(bf16[1,4,128,512]{3,2,1,0:T(8,128)(2,1)S(1)} %copy-done.3), channel_id=1, source_target_pairs={{0,28},{4,0},{8,4},{12,8},{16,12},{20,16},{24,20},{28,24},{1,29},{... | collective-permute-start | bytes 1572872 | tf_op jit(solution)/shard_map/ppermute | solution.py:10
  15.4 178.7 %collective-permute-start = (bf16[1,1,128,512]{3,2,1,0:T(8,128)(2,1)}, bf16[1,1,128,512]{3,2,1,0:T(8,128)(2,1)S(1)}, u32[]{:S(2)}, u32[]{:S(2)}) collective-permute-start(bf16[1,1,128,512]{3,2,1,0:T(8,128)(2,1)} %param.9), channel_id=1, source_target_pairs={{0,28},{4,0},{8,4},{12,8},{16,12},{20,16},{24,20},{28,24},{1,29},{... | collective-permute-start | bytes 393224 | tf_op jit(solution)/shard_map/ppermute | solution.py:10
  37.3 156.8 %all-to-all-start.1 = ((bf16[4,128,512]{2,1,0:T(8,128)(2,1)}), bf16[4,128,512]{2,1,0:T(8,128)(2,1)}, u32[]{:S(2)}, u32[]{:S(2)}) async-start(bf16[4,128,512]{2,1,0:T(8,128)(2,1)} %copy.32), calls=%async_computation.1 | async-start | bytes 1048576 | tf_op jit(solution)/shard_map/all_to_all | solution.py:36
  48.0 1.0 copy-start.1
  201.8 6.2 %collective-permute-start.2 = (bf16[128,512]{0,1:T(8,128)(2,1)S(1)}, bf16[128,512]{0,1:T(8,128)(2,1)S(1)}, u32[]{:S(2)}, u32[]{:S(2)}) collective-permute-start(bf16[128,512]{0,1:T(8,128)(2,1)S(1)} %maximum_bitcast_fusion), channel_id=1, source_target_pairs={{0,4},{4,8},{8,12},{12,16},{16,20},{20,24},{24,28},{28,0},{1,5},{5... | collective-permute-start | bytes 393224 | tf_op jit(solution)/shard_map/ppermute | solution.py:10
where the time goes:
time: 210 us; the launch traced here: 209 us
  other arithmetic  125 us (60%)
  waiting for transfers between devices  23.1 us (11%)
  local copies, waits for them, and re-layouts  23 us (11%)
  matrix products  20.5 us (10%)
  starting transfers between devices  14.2 us (7%)
  between operations  3.43 us (2%)
    another operation x14, other arithmetic, body(): jnp.linalg.cholesky(diag_blocks[0, 0].astype(jnp.float32) + block_sum(rec...  81 us
    another operation x3, other arithmetic, solve_panel(): return jax.scipy.linalg.solve_triangular(factor, total.T, lower=True).T  41.2 us
    another operation x12, local copies, waits for them, and re-layouts  14 us
    all_to_all x1, waiting for transfers between devices, body(): lax.all_to_all(send_diag, 'col', split_axis=0, concat_axis=0, tiled=True)  12.8 us
    ppermute x3, waiting for transfers between devices, from_behind(): return lax.ppermute(value, axis, pairs)  10.3 us
    dot_general x2, matrix products, block_sum(): jnp.einsum('cik,cjk->ij', left_slots, right_slots, preferred_element_type...  6.15 us
    another operation x6, matrix products, body(): jnp.linalg.cholesky(diag_blocks[0, 0].astype(jnp.float32) + block_sum(rec...  5.46 us
    all_to_all x1, starting transfers between devices, body(): lax.all_to_all(send_diag, 'col', split_axis=0, concat_axis=0, tiled=True)  5.29 us
  transfers between devices with their start and end apart: 5, of which 3 were waited for; matrix products, arithmetic and copies ran while one was open for 73% of the time, Pallas kernels for 0%

commit v1 on v0

--- a/solution.py
+++ b/solution.py
@@ -1,7 +1,131 @@
+import functools
+
 import jax
 import jax.numpy as jnp
 from jax import lax
+from jax.experimental import pallas as pl
+from jax.experimental.pallas import tpu as pltpu
 from jax.sharding import PartitionSpec as P
+
+TILE = 128
+SMALL = 16
+NT = (((1,), (1,)), ((), ()))
+TN = (((0,), (0,)), ((), ()))
+
+
+def split(value):
+    high = value.astype(jnp.bfloat16)
+    low = (value - high.astype(jnp.float32)).astype(jnp.bfloat16)
+    return high, low
+
+
+def dot(left, right, dims):
+    return lax.dot_general(left, right, dims, preferred_element_type=jnp.float32)
+
+
+def product(left, right, axis, dims):
+    left_high, left_low = split(left)
+    right_high, right_low = split(right)
+    return dot(
+        jnp.concatenate([left_high, left_high, left_low], axis=axis),
+        jnp.concatenate([right_high, right_low, right_high], axis=axis),
+        dims,
+    )
+
+
+def eliminate(work, spread):
+    full = (8, 2 * TILE)
+    lane = lax.broadcasted_iota(jnp.int32, (SMALL, TILE), 1)
+
+    def step(block, carry):
+        start = pl.multiple_of(block * SMALL, SMALL)
+        own = work.at[pl.ds(start, SMALL), :]
+        pivots = pltpu.roll(own[:, :TILE], lax.rem(TILE - start, TILE), 1)
+        for m in range(SMALL):
+            spread[m * SMALL : (m + 1) * SMALL, :] = jnp.broadcast_to(
+                pivots[:, m : m + 1], (SMALL, TILE)
+            )
+        value = {}
+        for m in range(SMALL):
+            for i in range(m, SMALL):
+                at = m * SMALL + i
+                value[i, m] = jnp.broadcast_to(spread[at : at + 1, :], (8, TILE))
+        rows = [jnp.broadcast_to(own[i : i + 1, :], full) for i in range(SMALL)]
+        for m in range(SMALL):
+            scale = lax.rsqrt(value[m, m])
+            rows[m] = rows[m] * jnp.concatenate([scale, scale], axis=1)
+            own[m : m + 1, :] = rows[m][0:1, :]
+            column = {i: value[i, m] * scale for i in range(m + 1, SMALL)}
+            for k in range(m + 1, SMALL):
+                for i in range(k, SMALL):
+                    value[i, k] = value[i, k] - column[i] * column[k]
+                rows[k] = rows[k] - jnp.concatenate([column[k], column[k]], axis=1) * rows[m]
+        solved = own[...]
+        high, low = split(solved)
+        left_high, left_low = split(jnp.where(lane >= start + SMALL, solved[:, :TILE], 0.0))
+        update = dot(
+            jnp.concatenate([left_high, left_high, left_low], axis=0),
+            jnp.concatenate([high, low, high], axis=0),
+            TN,
+        )
+        work[...] = work[...] - update
+        return carry
+
+    lax.fori_loop(0, TILE // SMALL, step, 0)
+
+
+def factor_kernel(x_ref, y_ref, diag_ref, panel_ref, factor_ref, solved_ref, total, work, spread):
+    sources, width, depth = x_ref.shape
+    height = y_ref.shape[1]
+    tiles = width // TILE
+    for q in range(tiles):
+        cols = slice(q * TILE, (q + 1) * TILE)
+        gram = diag_ref[q * TILE :, cols].astype(jnp.float32)
+        cross = panel_ref[:, cols].astype(jnp.float32)
+        for s in range(sources):
+            right = x_ref[s, cols, :]
+            gram = gram + dot(x_ref[s, q * TILE :, :], right, NT)
+            cross = cross + dot(y_ref[s], right, NT)
+        total[q * TILE : width, cols] = gram
+        total[width:, cols] = cross
+    row = lax.broadcasted_iota(jnp.int32, (TILE, TILE), 0)
+    lane = lax.broadcasted_iota(jnp.int32, (TILE, TILE), 1)
+    for q in range(tiles):
+        low, high = q * TILE, (q + 1) * TILE
+        work[:, :TILE] = total[low:high, low:high]
+        work[:, TILE:] = (row == lane).astype(jnp.float32)
+        eliminate(work, spread)
+        upper = jnp.where(row <= lane, work[:, :TILE], 0.0)
+        factor_ref[low:high, low:high] = upper.T.astype(jnp.bfloat16)
+        if q + 1 < tiles:
+            factor_ref[low:high, high:] = jnp.zeros((TILE, width - high), jnp.bfloat16)
+        below = product(total[high:, low:high], work[:, TILE:], 1, NT)
+        if q + 1 < tiles:
+            factor_ref[high:, low:high] = below[: width - high].astype(jnp.bfloat16)
+        solved_ref[:, low:high] = below[width - high :].astype(jnp.bfloat16)
+        if q + 1 < tiles:
+            total[high:, high:] = total[high:, high:] - product(below, below[: width - high], 1, NT)
+
+
+def factor_and_solve(x, y, diag, panel):
+    sources, width, depth = x.shape
+    height = y.shape[1]
+    vmem = pl.BlockSpec(memory_space=pltpu.VMEM)
+    return pl.pallas_call(
+        factor_kernel,
+        out_shape=(
+            jax.ShapeDtypeStruct((width, width), jnp.bfloat16),
+            jax.ShapeDtypeStruct((height, width), jnp.bfloat16),
+        ),
+        in_specs=[vmem] * 4,
+        out_specs=(vmem, vmem),
+        scratch_shapes=[
+            pltpu.VMEM((width + height, width), jnp.float32),
+            pltpu.VMEM((TILE, 2 * TILE), jnp.float32),
+            pltpu.VMEM((SMALL * SMALL, TILE), jnp.float32),
+        ],
+        compiler_params=pltpu.CompilerParams(vmem_limit_bytes=48 * 1024 * 1024),
+    )(x, y, diag, panel)
 
 
 def from_behind(value, axis, steps):
@@ -18,14 +142,6 @@
     return placed.astype(jnp.bfloat16)
 
 
-def block_sum(left_slots, right_slots):
-    return jnp.einsum("cik,cjk->ij", left_slots, right_slots, preferred_element_type=jnp.float32)
-
-
-def solve_panel(factor, total):
-    return jax.scipy.linalg.solve_triangular(factor, total.T, lower=True).T
-
-
 def body(diag_rows, next_rows, routes, diag_blocks, panel_blocks):
     columns = lax.axis_size("col")
     send_diag = place_slots(diag_rows[0], routes, columns)
@@ -35,13 +151,9 @@
         lax.all_to_all(send_diag, "col", split_axis=0, concat_axis=0, tiled=True),
         lax.all_to_all(send_next, "col", split_axis=0, concat_axis=0, tiled=True),
     )
-    factor = jnp.linalg.cholesky(
-        diag_blocks[0, 0].astype(jnp.float32) + block_sum(recv_diag, recv_diag)
-    )
-    total = panel_source[0, 0].astype(jnp.float32) + block_sum(recv_next, recv_diag)
-    solved = solve_panel(factor, total).astype(jnp.bfloat16)
+    factor, solved = factor_and_solve(recv_diag, recv_next, diag_blocks[0, 0], panel_source[0, 0])
     panel_out = from_behind(solved, "row", 1)
-    return (factor.astype(jnp.bfloat16)[None, None], panel_out[None, None])
+    return (factor[None, None], panel_out[None, None])
 
 
 def solution(mesh):

time: 210 us -> 88.5 us (0.42)
  other arithmetic: 125 us -> 0 us
  Pallas kernels: 0 us -> 27.7 us
  local copies, waits for them, and re-layouts: 23 us -> 4.88 us
  matrix products: 20.5 us -> 2.78 us
  waiting for transfers between devices: 23.1 us -> 37.1 us
  between operations: 3.43 us -> 0.69 us
    another operation x17 -> x0, other arithmetic: 122 us -> none  [the longest x14 81 us: body(): jnp.linalg.cholesky(diag_blocks[0, 0].astype(jnp.float32) + block_sum(rec...]
    pallas_call x0 -> x1, Pallas kernels: none -> 27.7 us  [factor_and_solve(): pl.pallas_call(factor_kernel, out_shape=(jax.ShapeDtypeStruct((width, wid...]
    another operation x17 -> x0, local copies, waits for them, and re-layouts: 14.7 us -> none
    another operation x13 -> x0, matrix products: 10.4 us -> none  [the longest x6 5.46 us: body(): jnp.linalg.cholesky(diag_blocks[0, 0].astype(jnp.float32) + block_sum(rec...]
    dot_general x2 -> x0, matrix products: 6.15 us -> none  [block_sum(): jnp.einsum('cik,cjk->ij', left_slots, right_slots, preferred_element_type...]
    all_to_all x1, waiting for transfers between devices: 12.8 us -> 18.1 us  [body(): lax.all_to_all(send_diag, 'col', split_axis=0, concat_axis=0, tiled=True)]
    ppermute x3, waiting for transfers between devices: 10.3 us -> 15.4 us  [from_behind(): return lax.ppermute(value, axis, pairs)]
    all_to_all x1, waiting for transfers between devices: 0.01 us -> 3.61 us  [body(): lax.all_to_all(send_next, 'col', split_axis=0, concat_axis=0, tiled=True)]
  transfers between devices with their start and end apart: 5 -> 5, of which waited for: 3 -> 5; matrix products, arithmetic and copies ran while one was open for 73% -> 4% of each run, Pallas kernels for 0% -> 0%
where the time goes in v1:
time: 88.5 us; the launch traced here: 88.2 us
  waiting for transfers between devices  37.1 us (42%)
  Pallas kernels  27.7 us (31%)
  starting transfers between devices  15.1 us (17%)
  local copies, waits for them, and re-layouts  4.88 us (6%)
  matrix products  2.78 us (3%)
    pallas_call x1, Pallas kernels, factor_and_solve(): pl.pallas_call(factor_kernel, out_shape=(jax.ShapeDtypeStruct((width, wid...  27.7 us
    all_to_all x1, waiting for transfers between devices, body(): lax.all_to_all(send_diag, 'col', split_axis=0, concat_axis=0, tiled=True)  18.1 us
    ppermute x3, waiting for transfers between devices, from_behind(): return lax.ppermute(value, axis, pairs)  15.4 us
    ppermute x3, starting transfers between devices, from_behind(): return lax.ppermute(value, axis, pairs)  6.93 us
    all_to_all x1, starting transfers between devices, body(): lax.all_to_all(send_diag, 'col', split_axis=0, concat_axis=0, tiled=True)  4.44 us
    all_to_all x1, starting transfers between devices, body(): lax.all_to_all(send_next, 'col', split_axis=0, concat_axis=0, tiled=True)  3.71 us
    all_to_all x1, waiting for transfers between devices, body(): lax.all_to_all(send_next, 'col', split_axis=0, concat_axis=0, tiled=True)  3.61 us
    dot_general x2, matrix products, place_slots(): jnp.einsum('sj,sab->jab', selector, sources, preferred_element_type=jnp.f...  2.78 us
  transfers between devices with their start and end apart: 5, of which 5 were waited for; matrix products, arithmetic and copies ran while one was open for 4% of the time, Pallas kernels for 0%

profile of v1, /device:TPU:0, one launch (start us, length us, event | category | flops | bytes accessed | tf_op | source)
XLA Modules:
  0.0 88.2 jit_solution(2518161620319998094)
XLA Ops:
  0.6 0.0 copy-start
  0.6 0.0 copy-start.2
  0.7 1.6 %copy.9 = bf16[1,4,128,512]{3,1,2,0:T(4,128)(2,1)S(1)} copy(bf16[1,4,128,512]{3,2,1,0:T(8,128)(2,1)} %param.6) | data formatting | bytes 1048576 | tf_op args[1]
  2.3 4.5 %collective-permute-start = (bf16[1,4,128,512]{3,1,2,0:T(4,128)(2,1)S(1)}, bf16[1,4,128,512]{3,1,2,0:T(4,128)(2,1)S(1)}, u32[]{:S(2)}, u32[]{:S(2)}) collective-permute-start(bf16[1,4,128,512]{3,1,2,0:T(4,128)(2,1)S(1)} %copy.9), channel_id=1, source_target_pairs={{0,28},{4,0},{8,4},{12,8},{16,12},{20,16},{24,20},{28,24},{1,29},{... | collective-permute-start | bytes 1572872 | tf_op jit(solution)/shard_map/ppermute | solution.py:134
  6.8 6.7 %collective-permute-done = bf16[1,4,128,512]{3,1,2,0:T(4,128)(2,1)S(1)} collective-permute-done((bf16[1,4,128,512]{3,1,2,0:T(4,128)(2,1)S(1)}, bf16[1,4,128,512]{3,1,2,0:T(4,128)(2,1)S(1)}, u32[]{:S(2)}, u32[]{:S(2)}) %collective-permute-start) | collective-permute-done | bytes 524320 | tf_op jit(solution)/shard_map/ppermute | solution.py:134
  13.5 1.1 %fusion.2 = bf16[4,128,512]{2,0,1:T(4,128)(2,1)S(1)} fusion(bf16[1,4,128,512]{3,1,2,0:T(4,128)(2,1)S(1)} %collective-permute-done, s32[4]{0:T(128)} %bitcast.17), kind=kOutput, calls=%fused_computation.4 | convolution fusion | flops 2097168 | bytes 1048592 | tf_op jit(solution)/shard_map/sj,sab->jab/dot_general | solution.py:141
  14.6 0.9 %copy.16 = bf16[4,128,512]{2,1,0:T(8,128)(2,1)} copy(bf16[4,128,512]{2,0,1:T(4,128)(2,1)S(1)} %fusion.2) | data formatting | bytes 1048576 | tf_op jit(solution)/shard_map/sj,sab->jab/dot_general | solution.py:141
  15.5 3.7 %all-to-all-start.1 = ((bf16[4,128,512]{2,1,0:T(8,128)(2,1)}), bf16[4,128,512]{2,1,0:T(8,128)(2,1)S(1)}, u32[]{:S(2)}, u32[]{:S(2)}) async-start(bf16[4,128,512]{2,1,0:T(8,128)(2,1)} %copy.16), calls=%async_computation.1 | async-start | bytes 1048576 | tf_op jit(solution)/shard_map/all_to_all | solution.py:152
  19.2 0.0 copy-done
  19.2 0.0 copy-done.2
  19.2 1.7 %fusion = bf16[4,512,512]{2,0,1:T(4,128)(2,1)S(1)} fusion(bf16[4,512,512]{2,1,0:T(8,128)(2,1)S(1)} %bitcast.13, s32[4]{0:T(128)S(1)} %bitcast.18), kind=kOutput, calls=%fused_computation.1 | convolution fusion | flops 8388624 | bytes 4194320 | tf_op jit(solution)/shard_map/sj,sab->jab/dot_general | solution.py:141
  20.9 1.7 %copy.15 = bf16[4,512,512]{2,1,0:T(8,128)(2,1)} copy(bf16[4,512,512]{2,0,1:T(4,128)(2,1)S(1)} %fusion) | data formatting | bytes 4194304 | tf_op jit(solution)/shard_map/sj,sab->jab/dot_general | solution.py:141
  22.6 0.0 copy-start.3
  22.6 0.0 copy-start.1
  22.6 3.6 %all-to-all-done.1.y_ref = bf16[4,128,512]{2,1,0:T(8,128)(2,1)S(1)} async-done(((bf16[4,128,512]{2,1,0:T(8,128)(2,1)}), bf16[4,128,512]{2,1,0:T(8,128)(2,1)S(1)}, u32[]{:S(2)}, u32[]{:S(2)}) %all-to-all-start.1) | async-done | bytes 524320 | tf_op jit(solution)/shard_map/all_to_all | solution.py:152
  26.2 4.4 %all-to-all-start = ((bf16[4,512,512]{2,1,0:T(8,128)(2,1)}), bf16[4,512,512]{2,1,0:T(8,128)(2,1)}, u32[]{:S(2)}, u32[]{:S(2)}) async-start(bf16[4,512,512]{2,1,0:T(8,128)(2,1)} %copy.15), calls=%async_computation | async-start | bytes 4194304 | tf_op jit(solution)/shard_map/all_to_all | solution.py:151
  30.7 0.0 copy-done.3
  30.7 2.4 %collective-permute-start.1 = (bf16[1,1,128,512]{3,2,1,0:T(8,128)(2,1)S(1)}, bf16[1,1,128,512]{3,2,1,0:T(8,128)(2,1)S(1)}, u32[]{:S(2)}, u32[]{:S(2)}) collective-permute-start(bf16[1,1,128,512]{3,2,1,0:T(8,128)(2,1)S(1)} %copy-done.3), channel_id=1, source_target_pairs={{0,28},{4,0},{8,4},{12,8},{16,12},{20,16},{24,20},{28,24},{1,29},{... | collective-permute-start | bytes 393224 | tf_op jit(solution)/shard_map/ppermute | solution.py:134
  33.1 2.5 %collective-permute-done.1 = bf16[1,1,128,512]{3,2,1,0:T(8,128)(2,1)S(1)} collective-permute-done((bf16[1,1,128,512]{3,2,1,0:T(8,128)(2,1)S(1)}, bf16[1,1,128,512]{3,2,1,0:T(8,128)(2,1)S(1)}, u32[]{:S(2)}, u32[]{:S(2)}) %collective-permute-start.1) | collective-permute-done | bytes 131104 | tf_op jit(solution)/shard_map/ppermute | solution.py:134
  35.6 18.1 %all-to-all-done.x_ref = bf16[4,512,512]{2,1,0:T(8,128)(2,1)} async-done(((bf16[4,512,512]{2,1,0:T(8,128)(2,1)}), bf16[4,512,512]{2,1,0:T(8,128)(2,1)}, u32[]{:S(2)}, u32[]{:S(2)}) %all-to-all-start) | async-done | bytes 2097184 | tf_op jit(solution)/shard_map/all_to_all | solution.py:151
  53.7 0.0 copy-done.1
  53.7 27.7 %shard_map.68 = (bf16[512,512]{1,0:T(8,128)(2,1)}, bf16[128,512]{1,0:T(8,128)(2,1)S(1)}) custom-call(bf16[4,512,512]{2,1,0:T(8,128)(2,1)} %all-to-all-done.x_ref, bf16[4,128,512]{2,1,0:T(8,128)(2,1)S(1)} %all-to-all-done.1.y_ref, bf16[512,512]{1,0:T(8,128)(2,1)S(1)} %bitcast.14, bf16[128,512]{1,0:T(8,128)(2,1)S(1)} %bitcast.15), custom_call_target="tpu_custom_call" | custom-call | tf_op jit(solution)/shard_map/pallas_call | solution.py:114
  81.4 0.0 collective-permute-start.2
  81.4 6.2 %collective-permute-done.2 = bf16[128,512]{1,0:T(8,128)(2,1)S(1)} collective-permute-done((bf16[128,512]{1,0:T(8,128)(2,1)S(1)}, bf16[128,512]{1,0:T(8,128)(2,1)S(1)}, u32[]{:S(2)}, u32[]{:S(2)}) %collective-permute-start.2) | collective-permute-done | bytes 131104 | tf_op jit(solution)/shard_map/ppermute | solution.py:134
  87.6 0.7 copy.18
Async XLA Ops:
  0.6 18.6 %copy-start = (bf16[1,4,512,512]{3,2,1,0:T(8,128)(2,1)S(1)}, bf16[1,4,512,512]{3,2,1,0:T(8,128)(2,1)}, u32[]{:S(2)}) copy-start(bf16[1,4,512,512]{3,2,1,0:T(8,128)(2,1)} %param.5) | copy-start | bytes 6291460
  0.6 18.5 %copy-start.2 = (s32[1,1,4]{2,1,0:T(1,128)S(1)}, s32[1,1,4]{2,1,0:T(1,128)}, u32[]{:S(2)}) copy-start(s32[1,1,4]{2,1,0:T(1,128)} %param.7) | copy-start | bytes 52
  2.3 11.2 %collective-permute-start = (bf16[1,4,128,512]{3,1,2,0:T(4,128)(2,1)S(1)}, bf16[1,4,128,512]{3,1,2,0:T(4,128)(2,1)S(1)}, u32[]{:S(2)}, u32[]{:S(2)}) collective-permute-start(bf16[1,4,128,512]{3,1,2,0:T(4,128)(2,1)S(1)} %copy.9), channel_id=1, source_target_pairs={{0,28},{4,0},{8,4},{12,8},{16,12},{20,16},{24,20},{28,24},{1,29},{... | collective-permute-start | bytes 1572872 | tf_op jit(solution)/shard_map/ppermute | solution.py:134
  15.5 10.8 %all-to-all-start.1 = ((bf16[4,128,512]{2,1,0:T(8,128)(2,1)}), bf16[4,128,512]{2,1,0:T(8,128)(2,1)S(1)}, u32[]{:S(2)}, u32[]{:S(2)}) async-start(bf16[4,128,512]{2,1,0:T(8,128)(2,1)} %copy.16), calls=%async_computation.1 | async-start | bytes 1048576 | tf_op jit(solution)/shard_map/all_to_all | solution.py:152
  22.6 8.1 %copy-start.3 = (bf16[1,1,128,512]{3,2,1,0:T(8,128)(2,1)S(1)}, bf16[1,1,128,512]{3,2,1,0:T(8,128)(2,1)}, u32[]{:S(2)}) copy-start(bf16[1,1,128,512]{3,2,1,0:T(8,128)(2,1)} %param.9) | copy-start | bytes 393220
  22.6 31.1 %copy-start.1 = (bf16[1,1,512,512]{3,2,1,0:T(8,128)(2,1)S(1)}, bf16[1,1,512,512]{3,2,1,0:T(8,128)(2,1)}, u32[]{:S(2)}) copy-start(bf16[1,1,512,512]{3,2,1,0:T(8,128)(2,1)} %param.8) | copy-start | bytes 1572868
  26.2 27.4 %all-to-all-start = ((bf16[4,512,512]{2,1,0:T(8,128)(2,1)}), bf16[4,512,512]{2,1,0:T(8,128)(2,1)}, u32[]{:S(2)}, u32[]{:S(2)}) async-start(bf16[4,512,512]{2,1,0:T(8,128)(2,1)} %copy.15), calls=%async_computation | async-start | bytes 4194304 | tf_op jit(solution)/shard_map/all_to_all | solution.py:151
  30.7 4.9 %collective-permute-start.1 = (bf16[1,1,128,512]{3,2,1,0:T(8,128)(2,1)S(1)}, bf16[1,1,128,512]{3,2,1,0:T(8,128)(2,1)S(1)}, u32[]{:S(2)}, u32[]{:S(2)}) collective-permute-start(bf16[1,1,128,512]{3,2,1,0:T(8,128)(2,1)S(1)} %copy-done.3), channel_id=1, source_target_pairs={{0,28},{4,0},{8,4},{12,8},{16,12},{20,16},{24,20},{28,24},{1,29},{... | collective-permute-start | bytes 393224 | tf_op jit(solution)/shard_map/ppermute | solution.py:134
  81.4 6.2 %collective-permute-start.2 = (bf16[128,512]{1,0:T(8,128)(2,1)S(1)}, bf16[128,512]{1,0:T(8,128)(2,1)S(1)}, u32[]{:S(2)}, u32[]{:S(2)}) collective-permute-start(bf16[128,512]{1,0:T(8,128)(2,1)S(1)} %get-tuple-element.5), channel_id=1, source_target_pairs={{0,4},{4,8},{8,12},{12,16},{16,20},{20,24},{24,28},{28,0},{1,5},{5... | collective-permute-start | bytes 393224 | tf_op jit(solution)/shard_map/ppermute | solution.py:134

commit v2 on v1

v2 whole, which is shorter than its diff:
```python
import jax
import jax.numpy as jnp
from jax import lax
from jax.experimental import pallas as pl
from jax.experimental.pallas import tpu as pltpu
from jax.sharding import PartitionSpec as P

TILE = 128
SMALL = 16
MESH = pl.DeviceIdType.MESH
NT = (((1,), (1,)), ((), ()))
TN = (((0,), (0,)), ((), ()))


def split(value):
    high = value.astype(jnp.bfloat16)
    low = (value - high.astype(jnp.float32)).astype(jnp.bfloat16)
    return high, low


def dot(left, right, dims):
    return lax.dot_general(left, right, dims, preferred_element_type=jnp.float32)


def product(left, right, axis, dims):
    left_high, left_low = split(left)
    right_high, right_low = split(right)
    return dot(
        jnp.concatenate([left_high, left_high, left_low], axis=axis),
        jnp.concatenate([right_high, right_low, right_high], axis=axis),
        dims,
    )


def eliminate(work, spread):
    full = (8, 2 * TILE)
    lane = lax.broadcasted_iota(jnp.int32, (SMALL, TILE), 1)

    def step(block, carry):
        start = pl.multiple_of(block * SMALL, SMALL)
        own = work.at[pl.ds(start, SMALL), :]
        pivots = pltpu.roll(own[:, :TILE], lax.rem(TILE - start, TILE), 1)
        for m in range(SMALL):
            spread[m * SMALL : (m + 1) * SMALL, :] = jnp.broadcast_to(
                pivots[:, m : m + 1], (SMALL, TILE)
            )
        value = {}
        for m in range(SMALL):
            for i in range(m, SMALL):
                at = m * SMALL + i
                value[i, m] = jnp.broadcast_to(spread[at : at + 1, :], (8, TILE))
        rows = [jnp.broadcast_to(own[i : i + 1, :], full) for i in range(SMALL)]
        for m in range(SMALL):
            scale = lax.rsqrt(value[m, m])
            rows[m] = rows[m] * jnp.concatenate([scale, scale], axis=1)
            own[m : m + 1, :] = rows[m][0:1, :]
            column = {i: value[i, m] * scale for i in range(m + 1, SMALL)}
            for k in range(m + 1, SMALL):
                for i in range(k, SMALL):
                    value[i, k] = value[i, k] - column[i] * column[k]
                rows[k] = rows[k] - jnp.concatenate([column[k], column[k]], axis=1) * rows[m]
        solved = own[...]
        high, low = split(solved)
        left_high, left_low = split(jnp.where(lane >= start + SMALL, solved[:, :TILE], 0.0))
        update = dot(
            jnp.concatenate([left_high, left_high, left_low], axis=0),
            jnp.concatenate([high, low, high], axis=0),
            TN,
        )
        work[...] = work[...] - update
        return carry

    lax.fori_loop(0, TILE // SMALL, step, 0)


def level_kernel(
    x_ref, y_ref, routes_ref, diag_ref, panel_ref, factor_ref, home_ref,
    x_send, x_recv, y_lift, y_send, y_recv, panel_recv, solved_send, solved_recv,
    total, inverse, work, spread,
    x_out, x_in, y_out, y_in, row_out, row_in, home_out, home_in,
):
    sources, width, depth = x_ref.shape
    tiles = width // TILE
    columns, rows = lax.axis_size("col"), lax.axis_size("row")
    my_column, my_row = lax.axis_index("col"), lax.axis_index("row")
    ahead, behind = lax.rem(my_row + 1, rows), lax.rem(my_row + rows - 1, rows)
    partner = [lax.rem(my_column + d, columns) for d in range(columns)]

    barrier = pltpu.get_barrier_semaphore()
    for d in range(1, columns):
        pl.semaphore_signal(barrier, inc=1, device_id={"col": partner[d]}, device_id_type=MESH)
    for other in (ahead, behind):
        pl.semaphore_signal(barrier, inc=1, device_id={"row": other}, device_id_type=MESH)

    slot = []
    for d in range(columns):
        found = jnp.int32(0)
        for s in range(sources):
            found = jnp.where(routes_ref[s] == partner[d], jnp.int32(s), found)
        slot.append(found)

    def chunk(q):
        return slice(q * TILE, (q + 1) * TILE)

    def stage(q):
        for d in range(1, columns):
            x_send[d - 1, chunk(q), :] = x_ref[slot[d], chunk(q), :]
        x_recv[0, chunk(q), :] = x_ref[slot[0], chunk(q), :]

    def remote(source, target, out, into, device):
        return pltpu.make_async_remote_copy(
            src_ref=source, dst_ref=target, send_sem=out, recv_sem=into,
            device_id=device, device_id_type=MESH,
        )

    x_copies = [
        [
            remote(
                x_send.at[d - 1, chunk(q), :], x_recv.at[d, chunk(q), :],
                x_out.at[q, d - 1], x_in.at[q, d - 1], {"col": partner[d]},
            )
            for d in range(1, columns)
        ]
        for q in range(tiles)
    ]
    lift = remote(y_ref, y_lift, row_out.at[0], row_in.at[0], {"row": behind})
    panel_copy = remote(panel_ref, panel_recv, row_out.at[1], row_in.at[1], {"row": behind})
    y_copies = [
        remote(y_send.at[d - 1], y_recv.at[d], y_out.at[d - 1], y_in.at[d - 1], {"col": partner[d]})
        for d in range(1, columns)
    ]
    home_copies = [
        remote(
            solved_send.at[q], solved_recv.at[q], home_out.at[q], home_in.at[q], {"row": ahead}
        )
        for q in range(tiles)
    ]

    stage(0)
    pl.semaphore_wait(barrier, columns + 1)
    for copy in x_copies[0]:
        copy.start()
    lift.start()
    panel_copy.start()
    for q in range(1, tiles):
        stage(q)
        for copy in x_copies[q]:
            copy.start()

    row = lax.broadcasted_iota(jnp.int32, (TILE, TILE), 0)
    lane = lax.broadcasted_iota(jnp.int32, (TILE, TILE), 1)
    for q in range(tiles):
        low, high = q * TILE, (q + 1) * TILE
        for copy in x_copies[q]:
            copy.wait_recv()
        gram = diag_ref[low:high, :high].astype(jnp.float32)
        for s in range(columns):
            gram = gram + dot(x_recv[s, low:high, :], x_recv[s, :high, :], NT)
        total[low:high, :high] = gram
        for p in range(q):
            left = product(total[low:high, chunk(p)], inverse[p], 1, NT)
            total[low:high, chunk(p)] = left
            factor_ref[low:high, chunk(p)] = left.astype(jnp.bfloat16)
            total[low:high, (p + 1) * TILE : high] = total[
                low:high, (p + 1) * TILE : high
            ] - product(left, total[(p + 1) * TILE : high, chunk(p)], 1, NT)
        work[:, :TILE] = total[low:high, low:high]
        work[:, TILE:] = (row == lane).astype(jnp.float32)
        eliminate(work, spread)
        upper = jnp.where(row <= lane, work[:, :TILE], 0.0)
        factor_ref[low:high, low:high] = upper.T.astype(jnp.bfloat16)
        if q + 1 < tiles:
            factor_ref[low:high, high:] = jnp.zeros((TILE, width - high), jnp.bfloat16)
        inverse[q] = work[:, TILE:]
        if q == 0:
            lift.wait_recv()
            for d in range(1, columns):
                y_send[d - 1] = y_lift[slot[d]]
                y_copies[d - 1].start()
            y_recv[0] = y_lift[slot[0]]

    panel_copy.wait_recv()
    for copy in y_copies:
        copy.wait_recv()
    cross = panel_recv[...].astype(jnp.float32)
    for s in range(columns):
        cross = cross + dot(y_recv[s], x_recv[s], NT)
    for q in range(tiles):
        solved = product(cross[:, :TILE], inverse[q], 1, NT)
        solved_send[q] = solved.astype(jnp.bfloat16)
        home_copies[q].start()
        if q + 1 < tiles:
            cross = cross[:, TILE:] - product(solved, total[(q + 1) * TILE :, chunk(q)], 1, NT)
    for q in range(tiles):
        home_copies[q].wait_recv()
        home_ref[:, chunk(q)] = solved_recv[q]

    for copy in [*sum(x_copies, []), lift, panel_copy, *y_copies, *home_copies]:
        copy.wait_send()


def body(diag_rows, next_rows, routes, diag_blocks, panel_blocks):
    x, y, diag, panel = diag_rows[0], next_rows[0], diag_blocks[0, 0], panel_blocks[0, 0]
    sources, width, depth = x.shape
    height = y.shape[1]
    columns = lax.axis_size("col")
    tiles = width // TILE
    kind = x.dtype
    vmem = pl.BlockSpec(memory_space=pltpu.VMEM)
    dma = pltpu.SemaphoreType.DMA
    factor, home = pl.pallas_call(
        level_kernel,
        out_shape=(
            jax.ShapeDtypeStruct((width, width), kind),
            jax.ShapeDtypeStruct((height, width), kind),
        ),
        in_specs=[vmem, vmem, pl.BlockSpec(memory_space=pltpu.SMEM), vmem, vmem],
        out_specs=(vmem, vmem),
        scratch_shapes=[
            pltpu.VMEM((columns - 1, width, depth), kind),
            pltpu.VMEM((columns, width, depth), kind),
            pltpu.VMEM((sources, height, depth), kind),
            pltpu.VMEM((columns - 1, height, depth), kind),
            pltpu.VMEM((columns, height, depth), kind),
            pltpu.VMEM((height, width), kind),
            pltpu.VMEM((tiles, height, TILE), kind),
            pltpu.VMEM((tiles, height, TILE), kind),
            pltpu.VMEM((width, width), jnp.float32),
            pltpu.VMEM((tiles, TILE, TILE), jnp.float32),
            pltpu.VMEM((TILE, 2 * TILE), jnp.float32),
            pltpu.VMEM((SMALL * SMALL, TILE), jnp.float32),
            dma((tiles, columns - 1)),
            dma((tiles, columns - 1)),
            dma((columns - 1,)),
            dma((columns - 1,)),
            dma((2,)),
            dma((2,)),
            dma((tiles,)),
            dma((tiles,)),
        ],
        compiler_params=pltpu.CompilerParams(
            collective_id=0, has_side_effects=True, vmem_limit_bytes=56 * 1024 * 1024
        ),
    )(x, y, routes[0, 0], diag, panel)
    return (factor[None, None], home[None, None])


def solution(mesh):
    placed = (
        P("row", "col", None, None),
        P("row", "col", None, None),
        P("row", "col", None),
        P("row", "col", None, None),
        P("row", "col", None, None),
    )
    return jax.shard_map(
        body,
        mesh=mesh,
        in_specs=placed,
        out_specs=(P("row", "col", None, None), P("row", "col", None, None)),
        check_vma=False,
    )
```

time: 88.5 us -> 50.7 us (0.57)
  waiting for transfers between devices: 37.1 us -> 0 us
  Pallas kernels: 27.7 us -> 46.5 us
  starting transfers between devices: 15.1 us -> 0 us
  matrix products: 2.78 us -> 0 us
  local copies, waits for them, and re-layouts: 4.88 us -> 3.44 us
    all_to_all x2 -> x0, waiting for transfers between devices: 21.7 us -> none  [the longest x1 18.1 us: body(): lax.all_to_all(send_diag, 'col', split_axis=0, concat_axis=0, tiled=True)]
    pallas_call x1, Pallas kernels: 27.7 us -> 46.5 us  [body(): pl.pallas_call(level_kernel, out_shape=(jax.ShapeDtypeStruct((width, widt...]
    ppermute x3 -> x0, waiting for transfers between devices: 15.4 us -> none  [from_behind(): return lax.ppermute(value, axis, pairs)]
    all_to_all x2 -> x0, starting transfers between devices: 8.15 us -> none  [the longest x1 4.44 us: body(): lax.all_to_all(send_diag, 'col', split_axis=0, concat_axis=0, tiled=True)]
    ppermute x3 -> x0, starting transfers between devices: 6.93 us -> none  [from_behind(): return lax.ppermute(value, axis, pairs)]
    dot_general x2 -> x0, matrix products: 2.78 us -> none  [place_slots(): jnp.einsum('sj,sab->jab', selector, sources, preferred_element_type=jnp.f...]
    dot_general x2 -> x0, local copies, waits for them, and re-layouts: 2.61 us -> none  [place_slots(): jnp.einsum('sj,sab->jab', selector, sources, preferred_element_type=jnp.f...]
    unnamed x10 -> x2, local copies, waits for them, and re-layouts: 2.27 us -> 3.44 us
  transfers between devices with their start and end apart: 5 -> 0, of which waited for: 5 -> 0; matrix products, arithmetic and copies ran while one was open for 4% -> 0% of each run, Pallas kernels for 0% -> 0%
where the time goes in v2:
time: 50.7 us; the launch traced here: 50.5 us
  Pallas kernels  46.5 us (92%)
  local copies, waits for them, and re-layouts  3.44 us (7%)
  between operations  0.64 us (1%)
    pallas_call x1, Pallas kernels, body(): pl.pallas_call(level_kernel, out_shape=(jax.ShapeDtypeStruct((width, widt...  46.5 us
    unnamed x2, local copies, waits for them, and re-layouts  3.44 us

profile of v2, /device:TPU:0, one launch (start us, length us, event | category | flops | bytes accessed | tf_op | source)
XLA Modules:
  0.0 50.5 jit_solution(3717388220564986724)
XLA Ops:
  0.6 46.5 %shard_map.68 = (bf16[512,512]{1,0:T(8,128)(2,1)}, bf16[128,512]{1,0:T(8,128)(2,1)}) custom-call(bf16[4,512,512]{2,1,0:T(8,128)(2,1)} %bitcast.7, bf16[4,128,512]{2,1,0:T(8,128)(2,1)} %bitcast.9, s32[4]{0:T(128)} %bitcast.13, bf16[512,512]{1,0:T(8,128)(2,1)} %bitcast.10, bf16[128,512]{1,0:T(8,128)(2,1)} %bitcast.11), custom_call_target="tpu_custom_call" | custom-call | tf_op jit(solution)/shard_map/pallas_call | solution.py:211
  47.1 1.9 %copy.9 = bf16[1,1,512,512]{3,2,1,0:T(8,128)(2,1)} copy(bf16[1,1,512,512]{3,2,1,0:T(8,128)(2,1)} %bitcast.8) | data formatting | bytes 1048576
  49.0 1.6 %copy.10 = bf16[1,1,128,512]{3,2,1,0:T(8,128)(2,1)} copy(bf16[1,1,128,512]{3,2,1,0:T(8,128)(2,1)} %bitcast.12) | data formatting | bytes 262144

commit v3 on v2

--- a/solution.py
+++ b/solution.py
@@ -7,6 +7,7 @@
 
 TILE = 128
 SMALL = 16
+HALF = SMALL // 2
 MESH = pl.DeviceIdType.MESH
 NT = (((1,), (1,)), ((), ()))
 TN = (((0,), (0,)), ((), ()))
@@ -33,32 +34,56 @@
 
 
 def eliminate(work, spread):
-    full = (8, 2 * TILE)
+    full = (HALF, 2 * TILE)
     lane = lax.broadcasted_iota(jnp.int32, (SMALL, TILE), 1)
 
     def step(block, carry):
         start = pl.multiple_of(block * SMALL, SMALL)
         own = work.at[pl.ds(start, SMALL), :]
         pivots = pltpu.roll(own[:, :TILE], lax.rem(TILE - start, TILE), 1)
+        tail = {}
+        lower = {}
         for m in range(SMALL):
-            spread[m * SMALL : (m + 1) * SMALL, :] = jnp.broadcast_to(
-                pivots[:, m : m + 1], (SMALL, TILE)
-            )
-        value = {}
-        for m in range(SMALL):
-            for i in range(m, SMALL):
-                at = m * SMALL + i
-                value[i, m] = jnp.broadcast_to(spread[at : at + 1, :], (8, TILE))
+            wide = jnp.broadcast_to(pivots[:, m : m + 1], (SMALL, TILE))
+            if m < HALF:
+                spread[m * SMALL : m * SMALL + HALF, :] = wide[:HALF]
+                lower[m] = wide[HALF:]
+            else:
+                tail[m] = wide[HALF:]
         rows = [jnp.broadcast_to(own[i : i + 1, :], full) for i in range(SMALL)]
-        for m in range(SMALL):
-            scale = lax.rsqrt(value[m, m])
-            rows[m] = rows[m] * jnp.concatenate([scale, scale], axis=1)
-            own[m : m + 1, :] = rows[m][0:1, :]
-            column = {i: value[i, m] * scale for i in range(m + 1, SMALL)}
-            for k in range(m + 1, SMALL):
-                for i in range(k, SMALL):
-                    value[i, k] = value[i, k] - column[i] * column[k]
-                rows[k] = rows[k] - jnp.concatenate([column[k], column[k]], axis=1) * rows[m]
+
+        def single(m, i):
+            at = m * SMALL + i
+            return jnp.broadcast_to(spread[at : at + 1, :], (HALF, TILE))
+
+        def twice(part):
+            return jnp.concatenate([part, part], axis=1)
+
+        for base in (0, HALF):
+            inside = range(base, base + HALF)
+            value = {(i, m): single(m, i) for m in inside for i in range(m, base + HALF)}
+            for m in inside:
+                scale = lax.rsqrt(value[m, m])
+                column = {i: value[i, m] * scale for i in range(m + 1, base + HALF)}
+                for k in column:
+                    for i in range(k, base + HALF):
+                        value[i, k] = value[i, k] - column[i] * column[k]
+                rows[m] = rows[m] * twice(scale)
+                own[m : m + 1, :] = rows[m][0:1, :]
+                for k in column:
+                    rows[k] = rows[k] - twice(column[k]) * rows[m]
+                if base == 0:
+                    lower[m] = lower[m] * scale
+                    spread[m * SMALL + HALF : (m + 1) * SMALL, :] = lower[m]
+                    for k in column:
+                        lower[k] = lower[k] - column[k] * lower[m]
+            if base == 0:
+                for k in range(HALF, SMALL):
+                    for m in range(HALF):
+                        across = single(m, k)
+                        tail[k] = tail[k] - across * lower[m]
+                        rows[k] = rows[k] - twice(across) * rows[m]
+                    spread[k * SMALL + HALF : (k + 1) * SMALL, :] = tail[k]
         solved = own[...]
         high, low = split(solved)
         left_high, left_low = split(jnp.where(lane >= start + SMALL, solved[:, :TILE], 0.0))
@@ -197,6 +222,17 @@
 
     for copy in [*sum(x_copies, []), lift, panel_copy, *y_copies, *home_copies]:
         copy.wait_send()
+
+
+def deliver_kernel(factor_ref, home_ref, factor_out, home_out, done):
+    copies = [
+        pltpu.make_async_copy(factor_ref, factor_out, done.at[0]),
+        pltpu.make_async_copy(home_ref, home_out, done.at[1]),
+    ]
+    for copy in copies:
+        copy.start()
+    for copy in copies:
+        copy.wait()
 
 
 def body(diag_rows, next_rows, routes, diag_blocks, panel_blocks):
@@ -242,6 +278,17 @@
             collective_id=0, has_side_effects=True, vmem_limit_bytes=56 * 1024 * 1024
         ),
     )(x, y, routes[0, 0], diag, panel)
+    anywhere = pl.BlockSpec(memory_space=pltpu.HBM)
+    factor, home = pl.pallas_call(
+        deliver_kernel,
+        out_shape=(
+            jax.ShapeDtypeStruct(factor.shape, kind),
+            jax.ShapeDtypeStruct(home.shape, kind),
+        ),
+        in_specs=[anywhere, anywhere],
+        out_specs=(anywhere, anywhere),
+        scratch_shapes=[dma((2,))],
+    )(factor, home)
     return (factor[None, None], home[None, None])
 
 

time: 50.7 us -> 65.4 us (1.29)
  Pallas kernels: 46.5 us -> 64.6 us
  local copies, waits for them, and re-layouts: 3.44 us -> 0 us
    pallas_call x0 -> x1, Pallas kernels: none -> 21 us  [body(): pl.pallas_call(deliver_kernel, out_shape=(jax.ShapeDtypeStruct(factor.sha...]
    unnamed x2 -> x0, local copies, waits for them, and re-layouts: 3.44 us -> none
    pallas_call x1, Pallas kernels: 46.5 us -> 43.7 us  [body(): pl.pallas_call(level_kernel, out_shape=(jax.ShapeDtypeStruct((width, widt...]
where the time goes in v3:
time: 65.4 us; the launch traced here: 65.3 us
  Pallas kernels  64.6 us (99%)
    pallas_call x1, Pallas kernels, body(): pl.pallas_call(level_kernel, out_shape=(jax.ShapeDtypeStruct((width, widt...  43.7 us
    pallas_call x1, Pallas kernels, body(): pl.pallas_call(deliver_kernel, out_shape=(jax.ShapeDtypeStruct(factor.sha...  21 us

profile of v3, /device:TPU:0, one launch (start us, length us, event | category | flops | bytes accessed | tf_op | source)
XLA Modules:
  0.0 65.3 jit_solution(9704015127690674420)
XLA Ops:
  0.6 43.7 %shard_map.68 = (bf16[512,512]{1,0:T(8,128)(2,1)}, bf16[128,512]{1,0:T(8,128)(2,1)}) custom-call(bf16[4,512,512]{2,1,0:T(8,128)(2,1)} %bitcast.7, bf16[4,128,512]{2,1,0:T(8,128)(2,1)} %bitcast.8, s32[4]{0:T(128)} %bitcast.11, bf16[512,512]{1,0:T(8,128)(2,1)} %bitcast.9, bf16[128,512]{1,0:T(8,128)(2,1)} %bitcast.10), custom_call_target="tpu_custom_call" | custom-call | tf_op jit(solution)/shard_map/pallas_call | solution.py:247
  44.3 21.0 %shard_map.69 = (bf16[512,512]{1,0:T(8,128)(2,1)}, bf16[128,512]{1,0:T(8,128)(2,1)}) custom-call(bf16[512,512]{1,0:T(8,128)(2,1)} %get-tuple-element.6.factor_ref, bf16[128,512]{1,0:T(8,128)(2,1)} %get-tuple-element.7.home_ref), custom_call_target="tpu_custom_call" | custom-call | tf_op jit(solution)/shard_map/pallas_call | solution.py:282

commit v4 on v3

--- a/solution.py
+++ b/solution.py
@@ -285,7 +285,7 @@
             jax.ShapeDtypeStruct(factor.shape, kind),
             jax.ShapeDtypeStruct(home.shape, kind),
         ),
-        in_specs=[anywhere, anywhere],
+        in_specs=[vmem, vmem],
         out_specs=(anywhere, anywhere),
         scratch_shapes=[dma((2,))],
     )(factor, home)

time: 65.4 us -> 46.4 us (0.71)
  Pallas kernels: 64.6 us -> 45.6 us
    pallas_call x1, Pallas kernels: 21 us -> 1.91 us  [body(): pl.pallas_call(deliver_kernel, out_shape=(jax.ShapeDtypeStruct(factor.sha...]
where the time goes in v4:
time: 46.4 us; the launch traced here: 46.2 us
  Pallas kernels  45.6 us (98%)
  between operations  0.64 us (1%)
    pallas_call x1, Pallas kernels, body(): pl.pallas_call(level_kernel, out_shape=(jax.ShapeDtypeStruct((width, widt...  43.7 us
    pallas_call x1, Pallas kernels, body(): pl.pallas_call(deliver_kernel, out_shape=(jax.ShapeDtypeStruct(factor.sha...  1.91 us

profile of v4, /device:TPU:0, one launch (start us, length us, event | category | flops | bytes accessed | tf_op | source)
XLA Modules:
  0.0 46.2 jit_solution(11761887531360597358)
XLA Ops:
  0.6 43.7 %shard_map.68 = (bf16[512,512]{1,0:T(8,128)(2,1)}, bf16[128,512]{1,0:T(8,128)(2,1)}) custom-call(bf16[4,512,512]{2,1,0:T(8,128)(2,1)} %bitcast.7, bf16[4,128,512]{2,1,0:T(8,128)(2,1)} %bitcast.8, s32[4]{0:T(128)} %bitcast.11, bf16[512,512]{1,0:T(8,128)(2,1)} %bitcast.9, bf16[128,512]{1,0:T(8,128)(2,1)} %bitcast.10), custom_call_target="tpu_custom_call" | custom-call | tf_op jit(solution)/shard_map/pallas_call | solution.py:247
  44.3 1.9 %shard_map.69 = (bf16[512,512]{1,0:T(8,128)(2,1)}, bf16[128,512]{1,0:T(8,128)(2,1)}) custom-call(bf16[512,512]{1,0:T(8,128)(2,1)} %get-tuple-element.6.factor_ref, bf16[128,512]{1,0:T(8,128)(2,1)} %get-tuple-element.7.home_ref), custom_call_target="tpu_custom_call" | custom-call | tf_op jit(solution)/shard_map/pallas_call | solution.py:282
